TPU v7x, 256 devices: a whole 4x4x8 slice. The times are simulated.
256 devices in a mesh: level: 8 (over y, core), row: 32 (over z, x).
Axes of the slice: x: 4, y: 4, z: 8, core: 2. Of those that a mesh axis runs over, the one named last changes fastest.
Arguments:
- points: float32 [8, 512, 3, 512], P('level', 'row'), may hold values from 0.02 to 4.5, as said below
- panels: float32 [8, 512, 512, 128], P('level', 'row'), may hold values from -6 to 6
- near_nodes: int32 [8, 512, 2], P('level', 'row'), may hold values from 0 to 47
- skeleton: int32 [8, 512, 128], P('level', 'row'), may hold values from 0 to 511, as said below
- owner_map: int32 [8, 512, 1], P('level', 'row'), may hold values from 0 to 31; in each aligned block of 16 rows (0 to 15, 16 to 31, ..., all dimensions but the last counted through in order) at most 2 rows name the same one
- transfer: float32 [8, 512, 128, 128], P('level', 'row'), may hold values from -0.375 to 0.375
- coupling: float32 [8, 4096, 128], P('level', 'row'), as said below
Outputs:
- solved: float32 [8, 512, 128, 128], P('level', 'row')
Inputs may be any that keep to these rules, and one draw needn't show every extreme that they name: `points`: channels 0 and 1 are plate positions, channel 2 is a positive film gap. `skeleton`: each node's 128 entries are distinct. `owner_map`: among the 16 nodes of one device, at most 2 have the same owner, and exactly 2 do for some owner. `coupling`: each 128-row block is symmetric and its diagonal exceeds the sum of the other magnitudes of its row by 0.5 or more.
All inputs are finite; a program needn't handle non-finite values.
Results may differ from a plain program's by a relative error of at most 0.0003.
Values sent between devices are 32-bit elements; how exact they have to be, the bound alone decides.
A program may use at most 128 MiB of HBM per device.

v0:
```python
import jax
import jax.numpy as jnp
from jax import lax
from jax.experimental import pallas as pl
from jax.experimental.pallas import tpu as pltpu
from jax.sharding import PartitionSpec as P
F32, BF16 = jnp.float32, jnp.bfloat16
NN, R, W = 16, 128, 32

def halves(x):
    high = x.astype(BF16)
    return high, (x - high.astype(F32)).astype(BF16)

def dot(a, b, dims=((1,), (0,))):
    return lax.dot_general(a, b, (dims, ((), ())), preferred_element_type=F32)

def spread_row(x, row):
    return jnp.broadcast_to(x[row:row + 1, :], x.shape)

def lane_pick(x, index):
    return jnp.take_along_axis(x, index, axis=1)

def invert_factors(diag, step):
    groups, parts = len(diag), W // 8
    lane = lax.broadcasted_iota(jnp.int32, (8, R), 1)
    row = lax.broadcasted_iota(jnp.int32, (8, R), 0)
    seg = (lane // W) * W
    within = lane % W
    rest = [list(d) for d in diag]
    work = [[jnp.where(within == row + 8 * q, 1.0, 0.0).astype(F32) for q in range(parts)] for _ in range(groups)]
    done = [[jnp.zeros((8, R), F32) for q in range(parts)] for _ in range(groups)]
    for j in range(0, W, step):
        q0 = j // 8
        for g in range(groups):
            cols = [{q: lane_pick(rest[g][q], seg + (j + t)) for q in range(q0, parts)} for t in range(step)]
            rows = [spread_row(rest[g][q0], (j + t) % 8) for t in range(step)]
            wrows = [spread_row(work[g][q0], (j + t) % 8) for t in range(step)]
            for t in range(step):
                at = (j + t) % 8
                scale = lax.rsqrt(spread_row(cols[t][q0], at))
                left = {q: cols[t][q] * scale for q in range(q0, parts)}
                right = rows[t] * scale
                wright = wrows[t] * scale
                for u in range(t + 1, step):
                    f = spread_row(left[q0], (j + u) % 8)
                    rows[u] = rows[u] - f * right
                    wrows[u] = wrows[u] - f * wright
                    for q in range(q0, parts):
                        cols[u][q] = cols[u][q] - left[q] * f
                done[g][q0] = jnp.where(row == at, wright, done[g][q0])
                for q in range(q0, parts):
                    l = jnp.where(row > at, left[q], 0.0) if q == q0 else left[q]
                    rest[g][q] = rest[g][q] - l * right
                    work[g][q] = work[g][q] - l * wright
    return done

def packed_coupling(s):
    row = lax.broadcasted_iota(jnp.int32, (64, R), 0)
    lane = lax.broadcasted_iota(jnp.int32, (64, R), 1)
    low, high = s[64:R, :], s[0:64, :]
    turned = pltpu.roll(high, 64, 1)
    body = jnp.where(lane - 64 > row, turned, jnp.where(lane - 64 == row, 0.5 * low, low))
    diagonal = jnp.sum(jnp.where(lane == row, 0.5 * high, 0.0), axis=0, keepdims=True)
    return body, jnp.broadcast_to(diagonal, (8, R))


def half_coupling(packed):
    row = lax.broadcasted_iota(jnp.int32, (64, R), 0)
    lane = lax.broadcasted_iota(jnp.int32, (64, R), 1)
    body = packed[0:64, :]
    turned = pltpu.roll(body, 64, 1)
    diagonal = jnp.broadcast_to(packed[64:65, :], (64, R))
    top = jnp.where(lane < 64, jnp.where(lane > row, turned, jnp.where(lane == row, diagonal, 0.0)), 0.0)
    low = jnp.where(lane - 64 <= row, body, 0.0)
    return jnp.concatenate([top, low], axis=0)


def eliminate(step, base, nodes, owner_ref, c_ref, spread, out_ref, hw):
    rows128 = lax.broadcasted_iota(jnp.int32, (R, R), 0)
    lanes128 = lax.broadcasted_iota(jnp.int32, (R, R), 1)
    eye = jnp.where(rows128 == lanes128, 1.0, 0.0).astype(F32)
    for n in range(nodes):
        ch, cl = halves(c_ref[base + n])
        gram = dot(jnp.concatenate([ch, ch, cl], 0), jnp.concatenate([ch, cl, ch], 0), ((0,), (0,)))
        owner = owner_ref[base + n]
        half = half_coupling(spread[owner % 4, owner // 4])
        hw[n, :, 0:R] = half + half.T + gram * (1.0 / R)
        hw[n, :, R:2 * R] = eye
    lane32 = lax.broadcasted_iota(jnp.int32, (W, R), 1) // W
    per = R // W
    groups = nodes // per
    for k in range(per):
        r0 = W * k
        diag = []
        for g in range(groups):
            packed = None
            for t in range(per):
                x = hw[per * g + t, r0:r0 + W, 0:R]
                if t != k:
                    x = pltpu.roll(x, (W * (t - k)) % R, 1)
                packed = x if packed is None else jnp.where(lane32 == t, x, packed)
            diag.append([packed[8 * q:8 * q + 8] for q in range(W // 8)])
        inv = invert_factors(diag, step)
        for g in range(groups):
            m = jnp.concatenate(inv[g], axis=0)
            md = jnp.concatenate([jnp.where(lane32 == t, m, 0.0) for t in range(per)], axis=0)
            mh, ml = halves(md)
            x = jnp.concatenate([hw[per * g + t, r0:r0 + W, :] for t in range(per)], axis=0)
            xh, xl = halves(x)
            x = dot(mh, xh) + (dot(mh, xl) + dot(ml, xh))
            xh, xl = halves(x)
            for t in range(per):
                n = per * g + t
                lo = slice(W * t, W * t + W)
                hw[n, r0:r0 + W, R:2 * R] = x[lo, R:]
                if k < per - 1:
                    lhs = jnp.concatenate([xh[lo, :R], xh[lo, :R], xl[lo, :R]], axis=0)
                    rhs = jnp.concatenate([xh[lo], xl[lo], xh[lo]], axis=0)
                    upd = dot(lhs, rhs, ((0,), (0,)))
                    hw[n, r0 + W:, :] = hw[n, r0 + W:, :] - upd[r0 + W:, :]
    for n in range(nodes):
        ch, cl = halves(c_ref[base + n])
        wh, wl = halves(hw[n, :, R:2 * R])
        both = dot(jnp.concatenate([ch, ch], 1), jnp.concatenate([wh, wl], 1), ((1,), (1,)))
        out_ref[base + n] = both + dot(cl, wh, ((1,), (1,)))


LEAF = 512
vm = pl.BlockSpec(memory_space=pltpu.VMEM)


def skeleton_points(points_ref, skeleton_ref, gathered):
    for n0 in range(0, NN, 8):
        at = skeleton_ref[n0:n0 + 8, :]
        inside, tile = at % R, at // R
        for c in range(3):
            got = None
            for t in range(LEAF // R):
                part = points_ref[c, n0:n0 + 8, t * R:(t + 1) * R]
                part = jnp.take_along_axis(part, inside, axis=1)
                got = part if got is None else jnp.where(tile == t, part, got)
            gathered[c, n0:n0 + 8, :] = got


def skeleton_columns(gathered, columns, base):
    for c in range(3):
        for n0 in range(0, NN, 8):
            turned = gathered[c, n0:n0 + 8, :].T
            for n in range(8):
                columns[base + n0 + n, c] = jnp.broadcast_to(turned[:, n:n + 1], (R, R))


def one_block(columns, rows_ref, split_ref, node, far):
    near_x, near_y, near_g = columns[node, 0], columns[node, 1], columns[node, 2]
    parts = []
    for t in range(LEAF // R):
        lanes = slice(t * R, (t + 1) * R)
        dx = near_x - rows_ref[far, 0:1, lanes]
        dy = near_y - rows_ref[far, 1:2, lanes]
        parts.append(lax.rsqrt(dx * dx + dy * dy + near_g * rows_ref[far, 2:3, lanes]))
    kh, kl = halves(jnp.concatenate(parts, axis=1))
    high = dot(kh, split_ref[far])
    return high[:, :R] + (high[:, R:] + dot(kl, split_ref[far, :, 0:R]))


def chosen_block(columns, rows_ref, split_ref, node, far, allowed):
    inside = (far >= 0) & (far < NN) & allowed
    block = one_block(columns, rows_ref, split_ref, node, jnp.where(inside, far, 0))
    return jnp.where(inside, block, 0.0)


MESH = pl.DeviceIdType.MESH
NX, NZ, PACK, GS = 4, 8, 72, 1
GROUPS = NN // GS
SCALE = LEAF ** (-0.5)


def to_row(source, target, send, recv, row):
    return pltpu.make_async_remote_copy(
        src_ref=source, dst_ref=target, send_sem=send, recv_sem=recv,
        device_id=(lax.axis_index("level"), row), device_id_type=MESH,
    )


def climb_kernel(owner_ref, points_hbm, skeleton_hbm, near_hbm, coupling_hbm, panels_hbm, transfer_hbm,
                 solved,
                 points, rows, skeleton, near, panels, split, transfer, wide, coupling, spread,
                 gathered, far_gathered, far_near_vmem, far_near, columns, lent, lent_in, below, carried, hw,
                 fetch_sem, near_sem, ask_send, ask_receive, halo_send, halo_receive, up_send, up_receive,
                 x_send, x_receive, z_send, z_receive):
    level, me = lax.axis_index("level"), lax.axis_index("row")
    top, count = lax.axis_size("level") - 1, NX * NZ
    z, x = me // NX, me % NX
    previous, following = (me + count - 1) % count, (me + 1) % count
    along_x = [z * NX + (x + d) % NX for d in range(1, NX)]
    along_z = [(z + d) % NZ * NX + x for d in range(1, NZ)]

    fetches = [
        pltpu.make_async_copy(source, target, fetch_sem.at[i])
        for i, (source, target) in enumerate(
            ((points_hbm, points), (skeleton_hbm, skeleton), (near_hbm, near), (coupling_hbm, coupling), (panels_hbm, panels), (transfer_hbm, transfer))
        )
    ]
    for copy in fetches:
        copy.start()

    barrier = pltpu.get_barrier_semaphore()
    peers = [(level, r) for r in [previous, following] + along_z + along_x]
    peers += [((level + top) % (top + 1), me), ((level + 1) % (top + 1), me)]
    for device in peers:
        pl.semaphore_signal(barrier, inc=1, device_id=device, device_id_type=MESH)

    for i in (0, 1, 3):
        fetches[i].wait()
    skeleton_points(points, skeleton, gathered)
    body, diagonal = packed_coupling(coupling[...])
    spread[x, z, 0:64, :] = body
    spread[x, z, 64:PACK, :] = diagonal
    pl.semaphore_wait(barrier, len(peers))

    asks = []
    for i, (source, target) in enumerate(((gathered, far_gathered), (near_hbm, far_near_vmem))):
        asks.append(to_row(source, target.at[0], ask_send.at[0, i], ask_receive.at[0, i], following))
        asks.append(to_row(source, target.at[1], ask_send.at[1, i], ask_receive.at[1, i], previous))
    column = [to_row(spread.at[x, z], spread.at[x, z], z_send.at[i], z_receive.at[i], r) for i, r in enumerate(along_z)]
    plane = [to_row(spread.at[x], spread.at[x], x_send.at[i], x_receive.at[i], r) for i, r in enumerate(along_x)]
    for copy in asks + column:
        copy.start()

    for n in range(NN):
        for c in range(3):
            rows[n, c:c + 1, :] = points[c, n:n + 1, :]
    skeleton_columns(gathered, columns, 2 * NN)
    fetches[2].wait()
    fetches[4].wait()

    def divide(n, carry):
        high, low = halves(panels[n])
        split[n] = jnp.concatenate([high, low], axis=1)
        return carry

    lax.fori_loop(0, NN, divide, 0)

    def own(i, carry):
        for u in range(4):
            n = 4 * i + u
            carried[n] = one_block(columns, rows, split, 2 * NN + n, n)
        return carry

    lax.fori_loop(0, NN // 4, own, 0)

    for copy in asks:
        copy.wait()
    turn = pltpu.make_async_copy(far_near_vmem, far_near, near_sem)
    turn.start()
    skeleton_columns(far_gathered.at[0], columns, 0)
    skeleton_columns(far_gathered.at[1], columns, NN)
    turn.wait()

    def halo(n, side):
        return to_row(lent.at[side, n], lent_in.at[side, n], halo_send.at[side, n], halo_receive.at[side, n],
                      following if side else previous)

    def lend(n, carry):
        for side, offset, allowed in ((0, 2 * NN, me > 0), (1, 0, me < count - 1)):
            total = None
            for slot in range(2):
                block = chosen_block(columns, rows, split, side * NN + n, far_near[side, slot, n] - offset, allowed)
                total = block if total is None else total + block
            lent[side, n] = total * SCALE
        halo(n, 0).start()
        halo(n, 1).start()
        return carry

    lax.fori_loop(0, NN, lend, 0)
    for copy in column:
        copy.wait()
    for copy in plane:
        copy.start()

    def near_own(i, carry):
        for u in range(2):
            n = 2 * i + u
            total = carried[n]
            for slot in range(2):
                total = total + chosen_block(columns, rows, split, 2 * NN + n, near[slot, n] - NN, True)
            carried[n] = total * SCALE
        return carry

    lax.fori_loop(0, NN // 2, near_own, 0)
    fetches[5].wait()

    def widen(n, carry):
        high, low = halves(transfer[n])
        wide[n] = jnp.concatenate([high, high, low], axis=1)
        return carry

    lax.fori_loop(0, NN, widen, 0)

    def up(g):
        part = pl.ds(g * GS, GS)
        return pltpu.make_async_remote_copy(
            src_ref=carried.at[part], dst_ref=below.at[part], send_sem=up_send.at[g], recv_sem=up_receive.at[g],
            device_id=(level + 1, me), device_id_type=MESH,
        )

    def climb(g, carry):
        for u in range(GS):
            n = g * GS + u
            halo(n, 0).wait_recv()
            halo(n, 1).wait_recv()
            carried[n] = carried[n] + lent_in[0, n] + lent_in[1, n]

        @pl.when(level > 0)
        def _():
            up(g).wait_recv()
            for u in range(GS):
                n = g * GS + u
                high, low = halves(below[n])
                carried[n] = carried[n] + dot(wide[n], jnp.concatenate([high, low, high], axis=0))

        @pl.when(level < top)
        def _():
            up(g).start()

        return carry

    lax.fori_loop(0, GROUPS, climb, 0)
    for copy in plane:
        copy.wait()
    eliminate(4, 0, NN, owner_ref, carried, spread, solved, hw)

    def settle(g, carry):
        for u in range(GS):
            halo(g * GS + u, 0).wait_send()
            halo(g * GS + u, 1).wait_send()

        @pl.when(level < top)
        def _():
            up(g).wait_send()

        return carry

    lax.fori_loop(0, GROUPS, settle, 0)


def climb_levels(owner, points, skeleton, near, coupling, panels, transfer):
    hbm = pl.BlockSpec(memory_space=pltpu.HBM)
    shape = jax.ShapeDtypeStruct
    dma = pltpu.SemaphoreType.DMA
    v = pltpu.VMEM
    return pl.pallas_call(
        climb_kernel,
        out_shape=shape((NN, R, R), F32),
        in_specs=[pl.BlockSpec(memory_space=pltpu.SMEM)] + [hbm] * 6,
        out_specs=vm,
        scratch_shapes=[
            v(points.shape, F32), v((NN, 3, LEAF), F32), v(skeleton.shape, jnp.int32), pltpu.SMEM(near.shape, jnp.int32), v(panels.shape, F32),
            v((NN, LEAF, 2 * R), BF16), v((NN, R, R), F32), v((NN, R, 3 * R), BF16), v((R, R), F32), v((NX, NZ, PACK, R), F32),
            v((3, NN, R), F32), v((2, 3, NN, R), F32), v((2,) + near.shape, jnp.int32),
            pltpu.SMEM((2,) + near.shape, jnp.int32), v((3 * NN, 3, R, R), F32),
            v((2, NN, R, R), F32), v((2, NN, R, R), F32), v((NN, R, R), F32),
            v((NN, R, R), F32), v((NN, R, 2 * R), F32),
            dma((6,)), dma, dma((2, 2)), dma((2, 2)), dma((2, NN)), dma((2, NN)), dma((GROUPS,)), dma((GROUPS,)),
            dma((NX - 1,)), dma((NX - 1,)), dma((NZ - 1,)), dma((NZ - 1,)),
        ],
        compiler_params=pltpu.CompilerParams(collective_id=0, has_side_effects=True, vmem_limit_bytes=58 << 20),
        name="climb",
    )(owner, points, skeleton, near, coupling, panels, transfer)


def per_device(points, panels, near_nodes, skeleton, owner_map, transfer, coupling):
    return climb_levels(
        owner_map[0, :, 0], points[0].transpose(1, 0, 2), skeleton[0], near_nodes[0].T, coupling[0], panels[0], transfer[0]
    )[None]


def solution(mesh):
    return jax.shard_map(
        per_device,
        mesh=mesh,
        in_specs=(
            P("level", "row", None, None),
            P("level", "row", None, None),
            P("level", "row", None),
            P("level", "row", None),
            P("level", "row", None),
            P("level", "row", None, None),
            P("level", "row", None),
        ),
        out_specs=P("level", "row", None, None),
        check_vma=False,
    )
```

profile of v0, /device:TPU:27, one launch (start us, length us, event | category | flops | bytes accessed | tf_op | source)
XLA Modules:
  0.0 75.3 jit_solution(9055462572141518122)
XLA Ops:
  0.0 73.0 %climb.1 = f32[16,128,128]{2,1,0:T(8,128)} custom-call(s32[16]{0:T(128)} %bitcast.19, f32[3,16,512]{2,1,0:T(8,128)} %bitcast.15, s32[16,128]{1,0:T(8,128)} %bitcast.17, s32[2,16]{1,0:T(2,128)} %bitcast.18, f32[128,128]{1,0:T(8,128)} %bitcast.16, f32[16,512,128]{2,1,0:T(8,128)} %bitcast.12, f32[16,128,128]{2,1,0:T(8,128)} %bitcast.14), custom_call_target="tpu_custom_call" | custom-call | tf_op jit(solution)/shard_map/climb/pallas_call | solution.py:352
  73.0 2.3 %copy.9 = f32[1,16,128,128]{3,2,1,0:T(8,128)} copy(f32[1,16,128,128]{3,2,1,0:T(8,128)} %bitcast.13) | data formatting | bytes 2097152
where the time goes:
time: 75.4 us; the launch traced here: 75.3 us
  Pallas kernels  73 us (97%)
  local copies, waits for them, and re-layouts  2.3 us (3%)
    pallas_call x1, Pallas kernels, climb_levels(): pl.pallas_call(climb_kernel, out_shape=shape((NN, R, R), F32), in_specs=[...  73 us
    unnamed x1, local copies, waits for them, and re-layouts  2.3 us

commit v1 on v0

--- a/solution.py
+++ b/solution.py
@@ -28,7 +28,6 @@
     within = lane % W
     rest = [list(d) for d in diag]
     work = [[jnp.where(within == row + 8 * q, 1.0, 0.0).astype(F32) for q in range(parts)] for _ in range(groups)]
-    done = [[jnp.zeros((8, R), F32) for q in range(parts)] for _ in range(groups)]
     for j in range(0, W, step):
         q0 = j // 8
         for g in range(groups):
@@ -47,12 +46,12 @@
                     wrows[u] = wrows[u] - f * wright
                     for q in range(q0, parts):
                         cols[u][q] = cols[u][q] - left[q] * f
-                done[g][q0] = jnp.where(row == at, wright, done[g][q0])
                 for q in range(q0, parts):
                     l = jnp.where(row > at, left[q], 0.0) if q == q0 else left[q]
                     rest[g][q] = rest[g][q] - l * right
                     work[g][q] = work[g][q] - l * wright
-    return done
+                work[g][q0] = jnp.where(row == at, wright, work[g][q0])
+    return work
 
 def packed_coupling(s):
     row = lax.broadcasted_iota(jnp.int32, (64, R), 0)
@@ -75,18 +74,15 @@
     return jnp.concatenate([top, low], axis=0)
 
 
-def eliminate(step, base, nodes, owner_ref, c_ref, spread, out_ref, hw):
-    rows128 = lax.broadcasted_iota(jnp.int32, (R, R), 0)
-    lanes128 = lax.broadcasted_iota(jnp.int32, (R, R), 1)
-    eye = jnp.where(rows128 == lanes128, 1.0, 0.0).astype(F32)
+def eliminate(step, base, nodes, owner_ref, c_ref, by_z, by_x, out_ref, hw):
     for n in range(nodes):
         ch, cl = halves(c_ref[base + n])
         gram = dot(jnp.concatenate([ch, ch, cl], 0), jnp.concatenate([ch, cl, ch], 0), ((0,), (0,)))
         owner = owner_ref[base + n]
-        half = half_coupling(spread[owner % 4, owner // 4])
-        hw[n, :, 0:R] = half + half.T + gram * (1.0 / R)
-        hw[n, :, R:2 * R] = eye
-    lane32 = lax.broadcasted_iota(jnp.int32, (W, R), 1) // W
+        half = half_coupling(jnp.concatenate([by_z[owner % 4, owner // 4], by_x[owner // 4, owner % 4]], axis=0))
+        hw[n] = half + half.T + gram * (1.0 / R)
+    lane = lax.broadcasted_iota(jnp.int32, (W, R), 1)
+    row = lax.broadcasted_iota(jnp.int32, (W, R), 0)
     per = R // W
     groups = nodes // per
     for k in range(per):
@@ -95,32 +91,35 @@
         for g in range(groups):
             packed = None
             for t in range(per):
-                x = hw[per * g + t, r0:r0 + W, 0:R]
+                x = hw[per * g + t, r0:r0 + W, :]
                 if t != k:
                     x = pltpu.roll(x, (W * (t - k)) % R, 1)
-                packed = x if packed is None else jnp.where(lane32 == t, x, packed)
+                packed = x if packed is None else jnp.where(lane // W == t, x, packed)
             diag.append([packed[8 * q:8 * q + 8] for q in range(W // 8)])
         inv = invert_factors(diag, step)
+        unit = jnp.where(lane - r0 == row, 1.0, 0.0).astype(F32)
         for g in range(groups):
             m = jnp.concatenate(inv[g], axis=0)
-            md = jnp.concatenate([jnp.where(lane32 == t, m, 0.0) for t in range(per)], axis=0)
+            md = jnp.concatenate([jnp.where(lane // W == t, m, 0.0) for t in range(per)], axis=0)
             mh, ml = halves(md)
-            x = jnp.concatenate([hw[per * g + t, r0:r0 + W, :] for t in range(per)], axis=0)
+            x = jnp.concatenate([jnp.where(lane // W == k, unit, hw[per * g + t, r0:r0 + W, :]) for t in range(per)], axis=0)
             xh, xl = halves(x)
-            x = dot(mh, xh) + (dot(mh, xl) + dot(ml, xh))
+            x = dot(jnp.concatenate([mh, mh], axis=1), jnp.concatenate([xh, xl], axis=0)) + dot(ml, xh)
             xh, xl = halves(x)
             for t in range(per):
                 n = per * g + t
                 lo = slice(W * t, W * t + W)
-                hw[n, r0:r0 + W, R:2 * R] = x[lo, R:]
+                hw[n, r0:r0 + W, :] = jnp.where(lane < r0 + W, x[lo], 0.0)
                 if k < per - 1:
-                    lhs = jnp.concatenate([xh[lo, :R], xh[lo, :R], xl[lo, :R]], axis=0)
+                    lhs = jnp.concatenate([xh[lo], xh[lo], xl[lo]], axis=0)
                     rhs = jnp.concatenate([xh[lo], xl[lo], xh[lo]], axis=0)
-                    upd = dot(lhs, rhs, ((0,), (0,)))
-                    hw[n, r0 + W:, :] = hw[n, r0 + W:, :] - upd[r0 + W:, :]
+                    upd = dot(lhs, rhs, ((0,), (0,)))[r0 + W:]
+                    rest = hw[n, r0 + W:, :]
+                    at = lax.broadcasted_iota(jnp.int32, rest.shape, 1) // W
+                    hw[n, r0 + W:, :] = jnp.where(at == k, 0.0, rest) - upd
     for n in range(nodes):
         ch, cl = halves(c_ref[base + n])
-        wh, wl = halves(hw[n, :, R:2 * R])
+        wh, wl = halves(hw[n])
         both = dot(jnp.concatenate([ch, ch], 1), jnp.concatenate([wh, wl], 1), ((1,), (1,)))
         out_ref[base + n] = both + dot(cl, wh, ((1,), (1,)))
 
@@ -170,8 +169,7 @@
 
 
 MESH = pl.DeviceIdType.MESH
-NX, NZ, PACK, GS = 4, 8, 72, 1
-GROUPS = NN // GS
+NX, NZ, PACK, CUT = 4, 8, 72, 56
 SCALE = LEAF ** (-0.5)
 
 
@@ -184,10 +182,11 @@
 
 def climb_kernel(owner_ref, points_hbm, skeleton_hbm, near_hbm, coupling_hbm, panels_hbm, transfer_hbm,
                  solved,
-                 points, rows, skeleton, near, panels, split, transfer, wide, coupling, spread,
-                 gathered, far_gathered, far_near_vmem, far_near, columns, lent, lent_in, below, carried, hw,
+                 points, rows, skeleton, near, panels, split, transfer, lower, wide, rise, coupling, by_z, by_x,
+                 gathered, far_gathered, far_near_vmem, far_near, columns, lent, lent_in, mate, below, base, carried, hw,
                  fetch_sem, near_sem, ask_send, ask_receive, halo_send, halo_receive, up_send, up_receive,
-                 x_send, x_receive, z_send, z_receive):
+                 pair_send, pair_receive, lower_send, lower_receive,
+                 x_send, x_receive, z_send, z_receive, xx_send, xx_receive, zz_send, zz_receive):
     level, me = lax.axis_index("level"), lax.axis_index("row")
     top, count = lax.axis_size("level") - 1, NX * NZ
     z, x = me // NX, me % NX
@@ -206,7 +205,8 @@
 
     barrier = pltpu.get_barrier_semaphore()
     peers = [(level, r) for r in [previous, following] + along_z + along_x]
-    peers += [((level + top) % (top + 1), me), ((level + 1) % (top + 1), me)]
+    peers += [((level + step) % (top + 1), me) for step in (1, 2, top - 1, top)]
+    odd = level % 2 == 1
     for device in peers:
         pl.semaphore_signal(barrier, inc=1, device_id=device, device_id_type=MESH)
 
@@ -214,18 +214,33 @@
         fetches[i].wait()
     skeleton_points(points, skeleton, gathered)
     body, diagonal = packed_coupling(coupling[...])
-    spread[x, z, 0:64, :] = body
-    spread[x, z, 64:PACK, :] = diagonal
+    by_z[x, z] = body[0:CUT, :]
+    by_x[z, x, 0:64 - CUT, :] = body[CUT:64, :]
+    by_x[z, x, 64 - CUT:PACK - CUT, :] = diagonal
     pl.semaphore_wait(barrier, len(peers))
 
     asks = []
     for i, (source, target) in enumerate(((gathered, far_gathered), (near_hbm, far_near_vmem))):
         asks.append(to_row(source, target.at[0], ask_send.at[0, i], ask_receive.at[0, i], following))
         asks.append(to_row(source, target.at[1], ask_send.at[1, i], ask_receive.at[1, i], previous))
-    column = [to_row(spread.at[x, z], spread.at[x, z], z_send.at[i], z_receive.at[i], r) for i, r in enumerate(along_z)]
-    plane = [to_row(spread.at[x], spread.at[x], x_send.at[i], x_receive.at[i], r) for i, r in enumerate(along_x)]
-    for copy in asks + column:
+    first = [to_row(by_z.at[x, z], by_z.at[x, z], z_send.at[i], z_receive.at[i], r) for i, r in enumerate(along_z)]
+    first += [to_row(by_x.at[z, x], by_x.at[z, x], x_send.at[i], x_receive.at[i], r) for i, r in enumerate(along_x)]
+    second = [to_row(by_z.at[x], by_z.at[x], xx_send.at[i], xx_receive.at[i], r) for i, r in enumerate(along_x)]
+    second += [to_row(by_x.at[z], by_x.at[z], zz_send.at[i], zz_receive.at[i], r) for i, r in enumerate(along_z)]
+    for copy in asks + first:
         copy.start()
+
+    def to_level(source, target, send, recv, step):
+        return pltpu.make_async_remote_copy(
+            src_ref=source, dst_ref=target, send_sem=send, recv_sem=recv,
+            device_id=(level + step, me), device_id_type=MESH,
+        )
+
+    hand_down = to_level(transfer_hbm, lower, lower_send, lower_receive, 1)
+
+    @pl.when(jnp.logical_not(odd))
+    def _():
+        hand_down.start()
 
     for n in range(NN):
         for c in range(3):
@@ -240,14 +255,6 @@
         return carry
 
     lax.fori_loop(0, NN, divide, 0)
-
-    def own(i, carry):
-        for u in range(4):
-            n = 4 * i + u
-            carried[n] = one_block(columns, rows, split, 2 * NN + n, n)
-        return carry
-
-    lax.fori_loop(0, NN // 4, own, 0)
 
     for copy in asks:
         copy.wait()
@@ -273,75 +280,116 @@
         return carry
 
     lax.fori_loop(0, NN, lend, 0)
-    for copy in column:
+    for copy in first:
         copy.wait()
-    for copy in plane:
+    for copy in second:
         copy.start()
 
-    def near_own(i, carry):
-        for u in range(2):
-            n = 2 * i + u
-            total = carried[n]
-            for slot in range(2):
-                total = total + chosen_block(columns, rows, split, 2 * NN + n, near[slot, n] - NN, True)
-            carried[n] = total * SCALE
-        return carry
-
-    lax.fori_loop(0, NN // 2, near_own, 0)
     fetches[5].wait()
 
     def widen(n, carry):
         high, low = halves(transfer[n])
         wide[n] = jnp.concatenate([high, high, low], axis=1)
+        rise[n] = wide[n]
         return carry
 
     lax.fori_loop(0, NN, widen, 0)
 
-    def up(g):
-        part = pl.ds(g * GS, GS)
-        return pltpu.make_async_remote_copy(
-            src_ref=carried.at[part], dst_ref=below.at[part], send_sem=up_send.at[g], recv_sem=up_receive.at[g],
-            device_id=(level + 1, me), device_id_type=MESH,
-        )
-
-    def climb(g, carry):
-        for u in range(GS):
-            n = g * GS + u
-            halo(n, 0).wait_recv()
-            halo(n, 1).wait_recv()
-            carried[n] = carried[n] + lent_in[0, n] + lent_in[1, n]
-
-        @pl.when(level > 0)
+    @pl.when(odd)
+    def _():
+        hand_down.wait_recv()
+
+        def both_levels(n, carry):
+            high, low = halves(lower[n])
+            high, low = halves(dot(wide[n], jnp.concatenate([high, low, high], axis=0)))
+            rise[n] = jnp.concatenate([high, high, low], axis=1)
+            return carry
+
+        lax.fori_loop(0, NN, both_levels, 0)
+
+    def pair(n):
+        return to_level(base.at[n], mate.at[n], pair_send.at[n], pair_receive.at[n], 1)
+
+    def up(n):
+        return to_level(carried.at[n], below.at[n], up_send.at[0, n], up_receive.at[n], 2)
+
+    def across(n):
+        return to_level(below.at[n], below.at[n], up_send.at[1, n], up_receive.at[n], -1)
+
+    def times(matrix, block):
+        high, low = halves(block)
+        return dot(matrix, jnp.concatenate([high, low, high], axis=0))
+
+    def climb(n, carry):
+        mine = one_block(columns, rows, split, 2 * NN + n, n)
+        for slot in range(2):
+            mine = mine + chosen_block(columns, rows, split, 2 * NN + n, near[slot, n] - NN, True)
+        mine = mine * SCALE
+        halo(n, 0).wait_recv()
+        halo(n, 1).wait_recv()
+        local = mine + lent_in[0, n] + lent_in[1, n]
+        base[n] = local
+        carried[n] = local
+
+        @pl.when(jnp.logical_not(odd))
         def _():
-            up(g).wait_recv()
-            for u in range(GS):
-                n = g * GS + u
-                high, low = halves(below[n])
-                carried[n] = carried[n] + dot(wide[n], jnp.concatenate([high, low, high], axis=0))
-
-        @pl.when(level < top)
+            pair(n).start()
+
+        @pl.when(odd)
         def _():
-            up(g).start()
-
-        return carry
-
-    lax.fori_loop(0, GROUPS, climb, 0)
-    for copy in plane:
+            pair(n).wait_recv()
+            carried[n] = carried[n] + times(wide[n], mate[n])
+
+            @pl.when(level >= 2)
+            def _():
+                up(n).wait_recv()
+                across(n).start()
+                carried[n] = carried[n] + times(rise[n], below[n])
+
+            @pl.when(level < top)
+            def _():
+                up(n).start()
+
+        return carry
+
+    def follow(n, carry):
+        up(n).wait_recv()
+        carried[n] = carried[n] + times(rise[n], below[n])
+        return carry
+
+    lax.fori_loop(0, NN, climb, 0)
+
+    @pl.when(jnp.logical_not(odd) & (level >= 2))
+    def _():
+        lax.fori_loop(0, NN, follow, 0)
+
+    for copy in second:
         copy.wait()
-    eliminate(4, 0, NN, owner_ref, carried, spread, solved, hw)
-
-    def settle(g, carry):
-        for u in range(GS):
-            halo(g * GS + u, 0).wait_send()
-            halo(g * GS + u, 1).wait_send()
-
-        @pl.when(level < top)
+    eliminate(8, 0, NN, owner_ref, carried, by_z, by_x, solved, hw)
+
+    def settle(n, carry):
+        halo(n, 0).wait_send()
+        halo(n, 1).wait_send()
+
+        @pl.when(jnp.logical_not(odd))
         def _():
-            up(g).wait_send()
-
-        return carry
-
-    lax.fori_loop(0, GROUPS, settle, 0)
+            pair(n).wait_send()
+
+        @pl.when(odd & (level < top))
+        def _():
+            up(n).wait_send()
+
+        @pl.when(odd & (level >= 2))
+        def _():
+            across(n).wait_send()
+
+        return carry
+
+    lax.fori_loop(0, NN, settle, 0)
+
+    @pl.when(jnp.logical_not(odd))
+    def _():
+        hand_down.wait_send()
 
 
 def climb_levels(owner, points, skeleton, near, coupling, panels, transfer):
@@ -356,12 +404,14 @@
         out_specs=vm,
         scratch_shapes=[
             v(points.shape, F32), v((NN, 3, LEAF), F32), v(skeleton.shape, jnp.int32), pltpu.SMEM(near.shape, jnp.int32), v(panels.shape, F32),
-            v((NN, LEAF, 2 * R), BF16), v((NN, R, R), F32), v((NN, R, 3 * R), BF16), v((R, R), F32), v((NX, NZ, PACK, R), F32),
+            v((NN, LEAF, 2 * R), BF16), v((NN, R, R), F32), v((NN, R, R), F32), v((NN, R, 3 * R), BF16), v((NN, R, 3 * R), BF16), v((R, R), F32),
+            v((NX, NZ, CUT, R), F32), v((NZ, NX, PACK - CUT, R), F32),
             v((3, NN, R), F32), v((2, 3, NN, R), F32), v((2,) + near.shape, jnp.int32),
             pltpu.SMEM((2,) + near.shape, jnp.int32), v((3 * NN, 3, R, R), F32),
-            v((2, NN, R, R), F32), v((2, NN, R, R), F32), v((NN, R, R), F32),
-            v((NN, R, R), F32), v((NN, R, 2 * R), F32),
-            dma((6,)), dma, dma((2, 2)), dma((2, 2)), dma((2, NN)), dma((2, NN)), dma((GROUPS,)), dma((GROUPS,)),
+            v((2, NN, R, R), F32), v((2, NN, R, R), F32), v((NN, R, R), F32), v((NN, R, R), F32),
+            v((NN, R, R), F32), v((NN, R, R), F32), v((NN, R, R), F32),
+            dma((6,)), dma, dma((2, 2)), dma((2, 2)), dma((2, NN)), dma((2, NN)), dma((2, NN)), dma((NN,)), dma((NN,)), dma((NN,)), dma, dma,
+            dma((NX - 1,)), dma((NX - 1,)), dma((NZ - 1,)), dma((NZ - 1,)),
             dma((NX - 1,)), dma((NX - 1,)), dma((NZ - 1,)), dma((NZ - 1,)),
         ],
         compiler_params=pltpu.CompilerParams(collective_id=0, has_side_effects=True, vmem_limit_bytes=58 << 20),

time: 75.4 us -> 70.7 us (0.938)
  the two profiles are of different devices: /device:TPU:27 before, /device:TPU:24 now
where the time goes in v1:
time: 70.7 us; the launch traced here: 70.6 us
  Pallas kernels  68.3 us (97%)
  local copies, waits for them, and re-layouts  2.3 us (3%)
    pallas_call x1, Pallas kernels, climb_levels(): pl.pallas_call(climb_kernel, out_shape=shape((NN, R, R), F32), in_specs=[...  68.3 us
    unnamed x1, local copies, waits for them, and re-layouts  2.3 us

profile of v1, /device:TPU:24, one launch (start us, length us, event | category | flops | bytes accessed | tf_op | source)
XLA Modules:
  0.0 70.6 jit_solution(3207355135737808811)
XLA Ops:
  0.0 68.3 %climb.1 = f32[16,128,128]{2,1,0:T(8,128)} custom-call(s32[16]{0:T(128)} %bitcast.19, f32[3,16,512]{2,1,0:T(8,128)} %bitcast.15, s32[16,128]{1,0:T(8,128)} %bitcast.17, s32[2,16]{1,0:T(2,128)} %bitcast.18, f32[128,128]{1,0:T(8,128)} %bitcast.16, f32[16,512,128]{2,1,0:T(8,128)} %bitcast.12, f32[16,128,128]{2,1,0:T(8,128)} %bitcast.14), custom_call_target="tpu_custom_call" | custom-call | tf_op jit(solution)/shard_map/climb/pallas_call | solution.py:400
  68.3 2.3 %copy.9 = f32[1,16,128,128]{3,2,1,0:T(8,128)} copy(f32[1,16,128,128]{3,2,1,0:T(8,128)} %bitcast.13) | data formatting | bytes 2097152
